TPU v7x, 32 devices: a whole 2x2x4 slice. The times are simulated.
32 devices in a mesh: groups: 2 (over y), row: 4 (over z), col: 4 (over x, core).
Axes of the slice: x: 2, y: 2, z: 4, core: 2. Of those that a mesh axis runs over, the one named last changes fastest.
Arguments:
- object_slices: bfloat16 [2, 2, 1024, 512], P(None, None, ('groups', 'row'), 'col'), parts along dimension 2, may hold values from -4 to 4
- probe: float32 [2, 384, 384], replicated, may hold values from -5 to 5
- measured: float32 [8, 4, 1, 384, 384], P(('groups', 'row'), 'col'), parts along dimension 0, may hold values from 0 to 2
- offsets: int32 [8, 4, 1, 2], P(('groups', 'row'), 'col'), parts along dimension 0, may hold values from 0 to 127
- owned: int32 [8, 4], P(('groups', 'row'), 'col'), parts along dimension 0, may hold values 0 or 1
Outputs:
- gradient: float32 [2, 2, 1024, 512], P(None, None, ('groups', 'row'), 'col'), parts along dimension 2
There are 2 independent parts, one for each index of `groups`. A program takes and returns all parts, laid end to end along the dimension named above; an argument that names none is the same for every part. Nothing has to cross between parts.
All inputs are finite; a program needn't handle non-finite values. No bound on the sum of `owned` on one device may be relied on, other than what follows from the above.
Results may differ from a plain program's by a relative error of at most 0.0065.
Values may be sent and summed in bfloat16 or wider, within the bound.
A program may use at most 64 MiB of HBM per device.

v0:
```python
import math

import jax
import jax.numpy as jnp
from jax import lax
from jax.sharding import PartitionSpec as P


def shifted(x, axis, by):
    peers = lax.axis_size(axis)
    pairs = [(i, i + by) for i in range(peers) if 0 <= i + by < peers]
    return lax.ppermute(x, axis, pairs)


def make_tables(length):
    counter = jnp.arange(length, dtype=jnp.int32)
    differ = (counter[:, None] - counter[None, :]) % length
    chirp = (differ * differ % (2 * length)).astype(jnp.float32) * (math.pi / length)
    product = counter[:, None] * counter[None, :] % length
    fourier = product.astype(jnp.float32) * (-2.0 * math.pi / length)
    scaling = 1.0 / math.sqrt(length)
    return (
        (jnp.cos(chirp) * scaling).astype(jnp.bfloat16),
        (jnp.sin(chirp) * scaling).astype(jnp.bfloat16),
        (jnp.cos(fourier) * scaling).astype(jnp.bfloat16),
        (jnp.sin(fourier) * scaling).astype(jnp.bfloat16),
    )


def matmul_half(left, right):
    return jnp.dot(left, right, preferred_element_type=jnp.float32)


def transform(wave_re, wave_im, table_re, table_im, parity):
    half_re = (matmul_half(table_re, wave_re) - parity * matmul_half(table_im, wave_im)).astype(
        jnp.bfloat16
    )
    half_im = (matmul_half(table_re, wave_im) + parity * matmul_half(table_im, wave_re)).astype(
        jnp.bfloat16
    )
    out_re = matmul_half(half_re, table_re) - parity * matmul_half(half_im, table_im)
    out_im = matmul_half(half_im, table_re) + parity * matmul_half(half_re, table_im)
    return (out_re, out_im)


def position_grad(patch, probe_re, probe_im, measure, tables):
    chirp_re, chirp_im, four_re, four_im = tables
    first_re, first_im, second_re, second_im = (patch[0, 0], patch[0, 1], patch[1, 0], patch[1, 1])
    psi_re = (probe_re * first_re - probe_im * first_im).astype(jnp.bfloat16)
    psi_im = (probe_re * first_im + probe_im * first_re).astype(jnp.bfloat16)
    phi_re, phi_im = transform(psi_re, psi_im, chirp_re, chirp_im, 1.0)
    exit_re = (phi_re * second_re - phi_im * second_im).astype(jnp.bfloat16)
    exit_im = (phi_re * second_im + phi_im * second_re).astype(jnp.bfloat16)
    wave_re, wave_im = transform(exit_re, exit_im, four_re, four_im, 1.0)
    magnitude = jnp.maximum(jnp.sqrt(wave_re * wave_re + wave_im * wave_im), 0.5)
    ratio = measure / magnitude
    resid_re = (wave_re - ratio * wave_re).astype(jnp.bfloat16)
    resid_im = (wave_im - ratio * wave_im).astype(jnp.bfloat16)
    back_re, back_im = transform(resid_re, resid_im, four_re, four_im, -1.0)
    grad_two_re = phi_re * back_re + phi_im * back_im
    grad_two_im = phi_re * back_im - phi_im * back_re
    gphi_re = (second_re * back_re + second_im * back_im).astype(jnp.bfloat16)
    gphi_im = (second_re * back_im - second_im * back_re).astype(jnp.bfloat16)
    front_re, front_im = transform(gphi_re, gphi_im, chirp_re, chirp_im, -1.0)
    grad_one_re = probe_re * front_re + probe_im * front_im
    grad_one_im = probe_re * front_im - probe_im * front_re
    return jnp.stack([jnp.stack([grad_one_re, grad_one_im]), jnp.stack([grad_two_re, grad_two_im])])


def take_band(stack, axis_dim, tile, distance):
    return lax.slice_in_dim(stack, (distance + 2) * tile, (distance + 3) * tile, axis=axis_dim)


def chain_pass(stack, axis_dim, tile, mover, far_mover):
    total = take_band(stack, axis_dim, tile, 0)
    for direction in (1, -1):
        moved = far_mover(take_band(stack, axis_dim, tile, 2 * direction), direction)
        carried = take_band(stack, axis_dim, tile, direction) + moved
        total = total + mover(carried, direction)
    return total


def strip_rows_move(block, distance):
    return shifted(block, "row", distance)


def block_cols_move(block, distance):
    return shifted(block, "col", distance)


def shards(object_slices, probe, measured, offsets, owned):
    tile = object_slices.shape[2]
    length = probe.shape[1]
    tables = make_tables(length)
    pieces = []
    for distance in (-2, -1, 0, 1, 2):
        if distance == 0:
            pieces.append(object_slices)
        else:
            pieces.append(shifted(object_slices, "row", -distance))
    strip = jnp.concatenate(pieces, axis=2)
    pieces = []
    for distance in (-2, -1, 0, 1, 2):
        if distance == 0:
            pieces.append(strip)
        else:
            pieces.append(shifted(strip, "col", -distance))
    region = jnp.concatenate(pieces, axis=3)
    start_base = 2 * tile - length // 2
    gradient = jnp.zeros((2, 2, 5 * tile, 5 * tile), jnp.float32)
    row_start = start_base + offsets[0, 0, 0, 0]
    col_start = start_base + offsets[0, 0, 0, 1]
    zero_index = jnp.zeros((), jnp.int32)
    starts = (zero_index, zero_index, row_start, col_start)
    patch = lax.dynamic_slice(region, starts, (2, 2, length, length)).astype(jnp.float32)
    grads = position_grad(patch, probe[0], probe[1], measured[0, 0, 0], tables)
    gradient = lax.dynamic_update_slice(gradient, grads, starts)
    summed = chain_pass(
        chain_pass(gradient, 2, tile, strip_rows_move, strip_rows_move),
        3,
        tile,
        block_cols_move,
        block_cols_move,
    )
    return summed * owned[0, 0].astype(jnp.float32)


def solution(mesh):
    in_specs = (
        P(None, None, ("groups", "row"), "col"),
        P(),
        P(("groups", "row"), "col", None, None, None),
        P(("groups", "row"), "col", None, None),
        P(("groups", "row"), "col"),
    )
    out_specs = P(None, None, ("groups", "row"), "col")
    return jax.shard_map(shards, mesh=mesh, in_specs=in_specs, out_specs=out_specs, check_vma=False)
```

profile of v0, /device:TPU:1, one launch (start us, length us, event | category | flops | bytes accessed | tf_op | source)
XLA Modules:
  0.0 279.2 jit_solution(15772921586985629033)
XLA Ops:
  0.0 5.2 %collective-permute-start = (bf16[2,2,128,128]{3,2,1,0:T(8,128)(2,1)}, bf16[2,2,128,128]{3,2,1,0:T(8,128)(2,1)S(1)}, u32[]{:S(2)}, u32[]{:S(2)}) collective-permute-start(bf16[2,2,128,128]{3,2,1,0:T(8,128)(2,1)} %param.5), channel_id=1, source_target_pairs={{0,8},{4,12},{1,9},{5,13},{2,10},{6,14},{3,11},{7,15},{16,24},{20,... | collective-permute-start | bytes 393224 | tf_op jit(solution)/shard_map/ppermute | solution.py:12
  5.2 3.2 %collective-permute-start.1 = (bf16[2,2,128,128]{3,2,1,0:T(8,128)(2,1)}, bf16[2,2,128,128]{3,2,1,0:T(8,128)(2,1)S(1)}, u32[]{:S(2)}, u32[]{:S(2)}) collective-permute-start(bf16[2,2,128,128]{3,2,1,0:T(8,128)(2,1)} %param.5), channel_id=1, source_target_pairs={{0,4},{4,8},{8,12},{1,5},{5,9},{9,13},{2,6},{6,10},{10,14},{3,7},{... | collective-permute-start | bytes 393224 | tf_op jit(solution)/shard_map/ppermute | solution.py:12
  20.4 5.7 %collective-permute-start.5 = (bf16[2,2,640,128]{3,2,1,0:T(8,128)(2,1)S(1)}, bf16[2,2,640,128]{3,2,1,0:T(8,128)(2,1)S(1)}, u32[]{:S(2)}, u32[]{:S(2)}) collective-permute-start(bf16[2,2,640,128]{3,2,1,0:T(8,128)(2,1)S(1)} %constant_dynamic-update-slice_fusion), channel_id=1, source_target_pairs={{0,1},{1,2},{2,3},{4,5},{5,6},{6,7},{8,9},{9,10},{10,11},{12,13},{... | collective-permute-start | bytes 1966088 | tf_op jit(solution)/shard_map/ppermute | solution.py:12
  33.9 8.1 %collective-permute-done.5 = bf16[2,2,640,128]{3,2,1,0:T(8,128)(2,1)S(1)} collective-permute-done((bf16[2,2,640,128]{3,2,1,0:T(8,128)(2,1)S(1)}, bf16[2,2,640,128]{3,2,1,0:T(8,128)(2,1)S(1)}, u32[]{:S(2)}, u32[]{:S(2)}) %collective-permute-start.5) | collective-permute-done | bytes 655392 | tf_op jit(solution)/shard_map/ppermute | solution.py:12
  42.3 4.8 %collective-permute-done.6 = bf16[2,2,640,128]{3,2,1,0:T(8,128)(2,1)S(1)} collective-permute-done((bf16[2,2,640,128]{3,2,1,0:T(8,128)(2,1)S(1)}, bf16[2,2,640,128]{3,2,1,0:T(8,128)(2,1)S(1)}, u32[]{:S(2)}, u32[]{:S(2)}) %collective-permute-start.6) | collective-permute-done | bytes 655392 | tf_op jit(solution)/shard_map/ppermute | solution.py:12
  47.3 3.9 %collective-permute-done.7 = bf16[2,2,640,128]{3,2,1,0:T(8,128)(2,1)S(1)} collective-permute-done((bf16[2,2,640,128]{3,2,1,0:T(8,128)(2,1)S(1)}, bf16[2,2,640,128]{3,2,1,0:T(8,128)(2,1)S(1)}, u32[]{:S(2)}, u32[]{:S(2)}) %collective-permute-start.7) | collective-permute-done | bytes 655392 | tf_op jit(solution)/shard_map/ppermute | solution.py:12
  52.1 3.6 %fusion.47 = f32[384,384]{1,0:T(8,128)S(1)} fusion(bf16[384,384]{1,0:T(8,128)(2,1)S(1)} %get-tuple-element.12), kind=kOutput, calls=%fused_computation.100 | convolution fusion | flops 115900416 | bytes 884736 | tf_op jit(solution)/shard_map/dot_general | solution.py:31
  55.7 3.6 %fusion.49 = f32[384,384]{1,0:T(8,128)S(1)} fusion(bf16[384,384]{1,0:T(8,128)(2,1)S(1)} %get-tuple-element.11), kind=kOutput, calls=%fused_computation.102 | convolution fusion | flops 115900416 | bytes 884736 | tf_op jit(solution)/shard_map/dot_general | solution.py:31
  62.4 3.4 %fusion.9 = bf16[384,384]{1,0:T(8,128)(2,1)S(1)} fusion(f32[384,384]{1,0:T(8,128)S(1)} %fusion.49, bf16[384,384]{1,0:T(8,128)(2,1)S(1)} %get-tuple-element.12), kind=kOutput, calls=%fused_computation.29 | convolution fusion | flops 116195328 | bytes 1179648 | tf_op jit(solution)/shard_map/dot_general | solution.py:31
  76.7 3.2 %fusion.55 = f32[384,384]{1,0:T(8,128)S(1)} fusion(bf16[384,384]{1,0:T(8,128)(2,1)S(1)} %get-tuple-element.9), kind=kOutput, calls=%fused_computation.108 | convolution fusion | flops 114868224 | bytes 884736 | tf_op jit(solution)/shard_map/dot_general | solution.py:31
  95.5 3.4 %fusion.24 = (bf16[384,384]{1,0:T(8,128)(2,1)S(1)}, bf16[384,384]{1,0:T(8,128)(2,1)S(1)}) fusion(f32[1,1,1,384,384]{4,3,2,1,0:T(8,128)S(1)} %copy-done.2, f32[384,384]{1,0:T(8,128)S(1)} %convolution_subtract_fusion, f32[384,384]{1,0:T(8,128)S(1)} %fusion.54, bf16[384,384]{1,0:T(8,128)(2,1)S(1)} %fusion.11), kind=kOutput, calls=%fused_computation.52 | convolution fusion | flops 116637696 | bytes 2654208 | tf_op jit(solution)/shard_map/dot_general | solution.py:31
  120.2 3.6 %fusion.45 = f32[384,384]{1,0:T(8,128)S(1)} fusion(bf16[384,384]{1,0:T(8,128)(2,1)S(1)} %get-tuple-element.8), kind=kOutput, calls=%fused_computation.98 | convolution fusion | flops 115900416 | bytes 884736 | tf_op jit(solution)/shard_map/dot_general | solution.py:31
  123.8 3.6 %fusion.43 = f32[384,384]{1,0:T(8,128)S(1)} fusion(bf16[384,384]{1,0:T(8,128)(2,1)S(1)} %get-tuple-element.7), kind=kOutput, calls=%fused_computation.96 | convolution fusion | flops 115900416 | bytes 884736 | tf_op jit(solution)/shard_map/dot_general | solution.py:31
  130.6 3.4 %fusion.16 = bf16[384,384]{1,0:T(8,128)(2,1)S(1)} fusion(f32[384,384]{1,0:T(8,128)S(1)} %fusion.43, bf16[384,384]{1,0:T(8,128)(2,1)S(1)} %get-tuple-element.8), kind=kOutput, calls=%fused_computation.36 | convolution fusion | flops 116342784 | bytes 1179648 | tf_op jit(solution)/shard_map/dot_general | solution.py:31
  145.3 3.2 %broadcast_in_dim.2 = f32[2,2,640,640]{3,2,1,0:T(8,128)} broadcast(f32[]{:T(128)} %constant.35.clone.1), dimensions={} | broadcast | bytes 6553604 | tf_op jit(solution)/shard_map/broadcast_in_dim | solution.py:110
  148.5 17.7 %dynamic_update_slice.3 = f32[2,2,640,640]{3,2,1,0:T(8,128)} dynamic-update-slice(f32[2,2,640,640]{3,2,1,0:T(8,128)} %broadcast_in_dim.2, f32[2,2,384,384]{3,2,1,0:T(8,128)S(1)} %pad_maximum_fusion, s32[]{:T(128)} %constant.37.clone.1, s32[]{:T(128)} %constant.37.clone.1, s32[]{:T(128)S(6)} %select_n.115, s32[]{:T(128)S(6)} %select_n.116) | dynamic-update-slice | bytes 4718596 | tf_op jit(solution)/shard_map/dynamic_update_slice | solution.py:117
  169.2 22.7 %collective-permute-done.8 = f32[2,2,128,640]{3,2,1,0:T(8,128)S(1)} collective-permute-done((f32[2,2,128,640]{3,2,1,0:T(8,128)S(1)}, f32[2,2,128,640]{3,2,1,0:T(8,128)S(1)}, u32[]{:S(2)}, u32[]{:S(2)}) %collective-permute-start.8) | collective-permute-done | bytes 1310752 | tf_op jit(solution)/shard_map/ppermute | solution.py:12
  195.2 4.8 %collective-permute-start.9 = (f32[2,2,128,640]{3,2,1,0:T(8,128)S(1)}, f32[2,2,128,640]{3,2,1,0:T(8,128)S(1)}, u32[]{:S(2)}, u32[]{:S(2)}) collective-permute-start(f32[2,2,128,640]{3,2,1,0:T(8,128)S(1)} %get-tuple-element.5), channel_id=1, source_target_pairs={{0,4},{4,8},{8,12},{1,5},{5,9},{9,13},{2,6},{6,10},{10,14},{3,7},{... | collective-permute-start | bytes 3932168 | tf_op jit(solution)/shard_map/ppermute | solution.py:12
  200.0 20.9 %collective-permute-done.10 = f32[2,2,128,640]{3,2,1,0:T(8,128)S(1)} collective-permute-done((f32[2,2,128,640]{3,2,1,0:T(8,128)S(1)}, f32[2,2,128,640]{3,2,1,0:T(8,128)S(1)}, u32[]{:S(2)}, u32[]{:S(2)}) %collective-permute-start.10) | collective-permute-done | bytes 1310752 | tf_op jit(solution)/shard_map/ppermute | solution.py:12
  223.7 24.4 %collective-permute-done.11 = f32[2,2,128,640]{3,2,1,0:T(8,128)S(1)} collective-permute-done((f32[2,2,128,640]{3,2,1,0:T(8,128)S(1)}, f32[2,2,128,640]{3,2,1,0:T(8,128)S(1)}, u32[]{:S(2)}, u32[]{:S(2)}) %collective-permute-start.11) | collective-permute-done | bytes 1310752 | tf_op jit(solution)/shard_map/ppermute | solution.py:12
  249.7 8.6 %collective-permute-start.12 = (f32[2,2,128,128]{3,2,1,0:T(8,128)S(1)}, f32[2,2,128,128]{3,2,1,0:T(8,128)S(1)}, u32[]{:S(2)}, u32[]{:S(2)}) collective-permute-start(f32[2,2,128,128]{3,2,1,0:T(8,128)S(1)} %slice.83), channel_id=1, source_target_pairs={{0,1},{1,2},{2,3},{4,5},{5,6},{6,7},{8,9},{9,10},{10,11},{12,13},{... | collective-permute-start | bytes 786440 | tf_op jit(solution)/shard_map/ppermute | solution.py:12
  258.4 3.3 %collective-permute-done.12 = f32[2,2,128,128]{3,2,1,0:T(8,128)S(1)} collective-permute-done((f32[2,2,128,128]{3,2,1,0:T(8,128)S(1)}, f32[2,2,128,128]{3,2,1,0:T(8,128)S(1)}, u32[]{:S(2)}, u32[]{:S(2)}) %collective-permute-start.12) | collective-permute-done | bytes 262176 | tf_op jit(solution)/shard_map/ppermute | solution.py:12
  263.7 4.4 %collective-permute-start.13 = (f32[2,2,128,128]{3,2,1,0:T(8,128)S(1)}, f32[2,2,128,128]{3,2,1,0:T(8,128)S(1)}, u32[]{:S(2)}, u32[]{:S(2)}) collective-permute-start(f32[2,2,128,128]{3,2,1,0:T(8,128)S(1)} %get-tuple-element.19), channel_id=1, source_target_pairs={{0,1},{1,2},{2,3},{4,5},{5,6},{6,7},{8,9},{9,10},{10,11},{12,13},{... | collective-permute-start | bytes 786440 | tf_op jit(solution)/shard_map/ppermute | solution.py:12
  272.8 5.1 %collective-permute-done.15 = f32[2,2,128,128]{3,2,1,0:T(8,128)S(1)} collective-permute-done((f32[2,2,128,128]{3,2,1,0:T(8,128)S(1)}, f32[2,2,128,128]{3,2,1,0:T(8,128)S(1)}, u32[]{:S(2)}, u32[]{:S(2)}) %collective-permute-start.15) | collective-permute-done | bytes 262176 | tf_op jit(solution)/shard_map/ppermute | solution.py:12
  (76 shorter events, 101.2 us)
Async XLA Ops:
  0.0 42.2 %copy-start.1 = (bf16[2,2,128,128]{3,2,1,0:T(8,128)(2,1)S(1)}, bf16[2,2,128,128]{3,2,1,0:T(8,128)(2,1)}, u32[]{:S(2)}) copy-start(bf16[2,2,128,128]{3,2,1,0:T(8,128)(2,1)} %param.5) | copy-start | bytes 393220
  0.0 11.0 %collective-permute-start = (bf16[2,2,128,128]{3,2,1,0:T(8,128)(2,1)}, bf16[2,2,128,128]{3,2,1,0:T(8,128)(2,1)S(1)}, u32[]{:S(2)}, u32[]{:S(2)}) collective-permute-start(bf16[2,2,128,128]{3,2,1,0:T(8,128)(2,1)} %param.5), channel_id=1, source_target_pairs={{0,8},{4,12},{1,9},{5,13},{2,10},{6,14},{3,11},{7,15},{16,24},{20,... | collective-permute-start | bytes 393224 | tf_op jit(solution)/shard_map/ppermute | solution.py:12
  5.2 5.8 %collective-permute-start.1 = (bf16[2,2,128,128]{3,2,1,0:T(8,128)(2,1)}, bf16[2,2,128,128]{3,2,1,0:T(8,128)(2,1)S(1)}, u32[]{:S(2)}, u32[]{:S(2)}) collective-permute-start(bf16[2,2,128,128]{3,2,1,0:T(8,128)(2,1)} %param.5), channel_id=1, source_target_pairs={{0,4},{4,8},{8,12},{1,5},{5,9},{9,13},{2,6},{6,10},{10,14},{3,7},{... | collective-permute-start | bytes 393224 | tf_op jit(solution)/shard_map/ppermute | solution.py:12
  8.4 5.9 %collective-permute-start.2 = (bf16[2,2,128,128]{3,2,1,0:T(8,128)(2,1)}, bf16[2,2,128,128]{3,2,1,0:T(8,128)(2,1)S(1)}, u32[]{:S(2)}, u32[]{:S(2)}) collective-permute-start(bf16[2,2,128,128]{3,2,1,0:T(8,128)(2,1)} %param.5), channel_id=1, source_target_pairs={{4,0},{8,4},{12,8},{5,1},{9,5},{13,9},{6,2},{10,6},{14,10},{7,3},{... | collective-permute-start | bytes 393224 | tf_op jit(solution)/shard_map/ppermute | solution.py:12
  9.7 7.6 %collective-permute-start.3 = (bf16[2,2,128,128]{3,2,1,0:T(8,128)(2,1)}, bf16[2,2,128,128]{3,2,1,0:T(8,128)(2,1)S(1)}, u32[]{:S(2)}, u32[]{:S(2)}) collective-permute-start(bf16[2,2,128,128]{3,2,1,0:T(8,128)(2,1)} %param.5), channel_id=1, source_target_pairs={{8,0},{12,4},{9,1},{13,5},{10,2},{14,6},{11,3},{15,7},{24,16},{28,... | collective-permute-start | bytes 393224 | tf_op jit(solution)/shard_map/ppermute | solution.py:12
  17.3 16.5 %collective-permute-start.4 = (bf16[2,2,640,128]{3,2,1,0:T(8,128)(2,1)S(1)}, bf16[2,2,640,128]{3,2,1,0:T(8,128)(2,1)S(1)}, u32[]{:S(2)}, u32[]{:S(2)}) collective-permute-start(bf16[2,2,640,128]{3,2,1,0:T(8,128)(2,1)S(1)} %constant_dynamic-update-slice_fusion), channel_id=1, source_target_pairs={{0,2},{1,3},{4,6},{5,7},{8,10},{9,11},{12,14},{13,15},{16,18},{17,... | collective-permute-start | bytes 1966088 | tf_op jit(solution)/shard_map/ppermute | solution.py:12
  20.4 21.5 %collective-permute-start.5 = (bf16[2,2,640,128]{3,2,1,0:T(8,128)(2,1)S(1)}, bf16[2,2,640,128]{3,2,1,0:T(8,128)(2,1)S(1)}, u32[]{:S(2)}, u32[]{:S(2)}) collective-permute-start(bf16[2,2,640,128]{3,2,1,0:T(8,128)(2,1)S(1)} %constant_dynamic-update-slice_fusion), channel_id=1, source_target_pairs={{0,1},{1,2},{2,3},{4,5},{5,6},{6,7},{8,9},{9,10},{10,11},{12,13},{... | collective-permute-start | bytes 1966088 | tf_op jit(solution)/shard_map/ppermute | solution.py:12
  30.0 17.0 %collective-permute-start.6 = (bf16[2,2,640,128]{3,2,1,0:T(8,128)(2,1)S(1)}, bf16[2,2,640,128]{3,2,1,0:T(8,128)(2,1)S(1)}, u32[]{:S(2)}, u32[]{:S(2)}) collective-permute-start(bf16[2,2,640,128]{3,2,1,0:T(8,128)(2,1)S(1)} %constant_dynamic-update-slice_fusion), channel_id=1, source_target_pairs={{1,0},{2,1},{3,2},{5,4},{6,5},{7,6},{9,8},{10,9},{11,10},{13,12},{... | collective-permute-start | bytes 1966088 | tf_op jit(solution)/shard_map/ppermute | solution.py:12
  32.4 18.7 %collective-permute-start.7 = (bf16[2,2,640,128]{3,2,1,0:T(8,128)(2,1)S(1)}, bf16[2,2,640,128]{3,2,1,0:T(8,128)(2,1)S(1)}, u32[]{:S(2)}, u32[]{:S(2)}) collective-permute-start(bf16[2,2,640,128]{3,2,1,0:T(8,128)(2,1)S(1)} %constant_dynamic-update-slice_fusion), channel_id=1, source_target_pairs={{2,0},{3,1},{6,4},{7,5},{10,8},{11,9},{14,12},{15,13},{18,16},{19,... | collective-permute-start | bytes 1966088 | tf_op jit(solution)/shard_map/ppermute | solution.py:12
  47.2 4.7 %copy-start = (f32[2,384,384]{2,1,0:T(8,128)S(1)}, f32[2,384,384]{2,1,0:T(8,128)}, u32[]{:S(2)}) copy-start(f32[2,384,384]{2,1,0:T(8,128)} %param.6) | copy-start | bytes 3538948
  90.5 4.9 %copy-start.2 = (f32[1,1,1,384,384]{4,3,2,1,0:T(8,128)S(1)}, f32[1,1,1,384,384]{4,3,2,1,0:T(8,128)}, u32[]{:S(2)}) copy-start(f32[1,1,1,384,384]{4,3,2,1,0:T(8,128)} %param.7) | copy-start | bytes 1769476
  167.7 24.2 %collective-permute-start.8 = (f32[2,2,128,640]{3,2,1,0:T(8,128)S(1)}, f32[2,2,128,640]{3,2,1,0:T(8,128)S(1)}, u32[]{:S(2)}, u32[]{:S(2)}) collective-permute-start(f32[2,2,128,640]{3,2,1,0:T(8,128)S(1)} %slice.78), channel_id=1, source_target_pairs={{0,4},{4,8},{8,12},{1,5},{5,9},{9,13},{2,6},{6,10},{10,14},{3,7},{... | collective-permute-start | bytes 3932168 | tf_op jit(solution)/shard_map/ppermute | solution.py:12
  193.9 27.0 %collective-permute-start.10 = (f32[2,2,128,640]{3,2,1,0:T(8,128)S(1)}, f32[2,2,128,640]{3,2,1,0:T(8,128)S(1)}, u32[]{:S(2)}, u32[]{:S(2)}) collective-permute-start(f32[2,2,128,640]{3,2,1,0:T(8,128)S(1)} %get-tuple-element.6), channel_id=1, source_target_pairs={{4,0},{8,4},{12,8},{5,1},{9,5},{13,9},{6,2},{10,6},{14,10},{7,3},{... | collective-permute-start | bytes 3932168 | tf_op jit(solution)/shard_map/ppermute | solution.py:12
  195.2 28.5 %collective-permute-start.9 = (f32[2,2,128,640]{3,2,1,0:T(8,128)S(1)}, f32[2,2,128,640]{3,2,1,0:T(8,128)S(1)}, u32[]{:S(2)}, u32[]{:S(2)}) collective-permute-start(f32[2,2,128,640]{3,2,1,0:T(8,128)S(1)} %get-tuple-element.5), channel_id=1, source_target_pairs={{0,4},{4,8},{8,12},{1,5},{5,9},{9,13},{2,6},{6,10},{10,14},{3,7},{... | collective-permute-start | bytes 3932168 | tf_op jit(solution)/shard_map/ppermute | solution.py:12
  222.4 25.7 %collective-permute-start.11 = (f32[2,2,128,640]{3,2,1,0:T(8,128)S(1)}, f32[2,2,128,640]{3,2,1,0:T(8,128)S(1)}, u32[]{:S(2)}, u32[]{:S(2)}) collective-permute-start(f32[2,2,128,640]{3,2,1,0:T(8,128)S(1)} %slice_add_fusion), channel_id=1, source_target_pairs={{4,0},{8,4},{12,8},{5,1},{9,5},{13,9},{6,2},{10,6},{14,10},{7,3},{... | collective-permute-start | bytes 3932168 | tf_op jit(solution)/shard_map/ppermute | solution.py:12
  249.7 11.9 %collective-permute-start.12 = (f32[2,2,128,128]{3,2,1,0:T(8,128)S(1)}, f32[2,2,128,128]{3,2,1,0:T(8,128)S(1)}, u32[]{:S(2)}, u32[]{:S(2)}) collective-permute-start(f32[2,2,128,128]{3,2,1,0:T(8,128)S(1)} %slice.83), channel_id=1, source_target_pairs={{0,1},{1,2},{2,3},{4,5},{5,6},{6,7},{8,9},{9,10},{10,11},{12,13},{... | collective-permute-start | bytes 786440 | tf_op jit(solution)/shard_map/ppermute | solution.py:12
  261.7 8.4 %collective-permute-start.14 = (f32[2,2,128,128]{3,2,1,0:T(8,128)S(1)}, f32[2,2,128,128]{3,2,1,0:T(8,128)S(1)}, u32[]{:S(2)}, u32[]{:S(2)}) collective-permute-start(f32[2,2,128,128]{3,2,1,0:T(8,128)S(1)} %get-tuple-element.20), channel_id=1, source_target_pairs={{1,0},{2,1},{3,2},{5,4},{6,5},{7,6},{9,8},{10,9},{11,10},{13,12},{... | collective-permute-start | bytes 786440 | tf_op jit(solution)/shard_map/ppermute | solution.py:12
  263.7 9.1 %collective-permute-start.13 = (f32[2,2,128,128]{3,2,1,0:T(8,128)S(1)}, f32[2,2,128,128]{3,2,1,0:T(8,128)S(1)}, u32[]{:S(2)}, u32[]{:S(2)}) collective-permute-start(f32[2,2,128,128]{3,2,1,0:T(8,128)S(1)} %get-tuple-element.19), channel_id=1, source_target_pairs={{0,1},{1,2},{2,3},{4,5},{5,6},{6,7},{8,9},{9,10},{10,11},{12,13},{... | collective-permute-start | bytes 786440 | tf_op jit(solution)/shard_map/ppermute | solution.py:12
  270.2 7.7 %collective-permute-start.15 = (f32[2,2,128,128]{3,2,1,0:T(8,128)S(1)}, f32[2,2,128,128]{3,2,1,0:T(8,128)S(1)}, u32[]{:S(2)}, u32[]{:S(2)}) collective-permute-start(f32[2,2,128,128]{3,2,1,0:T(8,128)S(1)} %slice_add_fusion.3), channel_id=1, source_target_pairs={{1,0},{2,1},{3,2},{5,4},{6,5},{7,6},{9,8},{10,9},{11,10},{13,12},{... | collective-permute-start | bytes 786440 | tf_op jit(solution)/shard_map/ppermute | solution.py:12
where the time goes:
time: 285 us; the launch traced here: 279 us
  waiting for transfers between devices  100 us (35%)
  matrix products  92.3 us (32%)
  starting transfers between devices  49.3 us (17%)
  local copies, waits for them, and re-layouts  25.4 us (9%)
  other arithmetic  7.42 us (3%)
  between operations  4.31 us (2%)
    ppermute x16, waiting for transfers between devices, shifted(): return lax.ppermute(x, axis, pairs)  100 us
    dot_general x32, matrix products, matmul_half(): return jnp.dot(left, right, preferred_element_type=jnp.float32)  92.3 us
    ppermute x16, starting transfers between devices, shifted(): return lax.ppermute(x, axis, pairs)  49.3 us
    dynamic_update_slice x1, local copies, waits for them, and re-layouts, shards(): gradient = lax.dynamic_update_slice(gradient, grads, starts)  17.7 us
  transfers between devices with their start and end apart: 16, of which 11 were waited for; matrix products, arithmetic and copies ran while one was open for 2% of the time, Pallas kernels for 0%

commit v1 on v0

v1 whole, which is shorter than its diff:
```python
import functools
import math

import jax
import jax.numpy as jnp
import numpy as np
from jax import lax
from jax.experimental import pallas as pl
from jax.experimental.pallas import tpu as pltpu
from jax.sharding import PartitionSpec as P

MESH = pl.DeviceIdType.MESH
F32 = jnp.float32
BF16 = jnp.bfloat16
STEPS = (-2, -1, 1, 2)


def make_tables(length):
    counter = np.arange(length, dtype=np.int32)
    differ = (counter[:, None] - counter[None, :]) % length
    chirp = (differ * differ % (2 * length)).astype(np.float32) * np.float32(math.pi / length)
    product = counter[:, None] * counter[None, :] % length
    fourier = product.astype(np.float32) * np.float32(-2.0 * math.pi / length)
    scaling = np.float32(1.0 / math.sqrt(length))
    parts = (np.cos(chirp), np.sin(chirp), np.cos(fourier), np.sin(fourier))
    return [jnp.asarray(part * scaling, BF16) for part in parts]


def kernel(
    n_row, n_col, tile, length,
    offs_ref, owned_ref, obj_ref, probe_ref, meas_ref, hre_ref, him_ref, fre_ref, fim_ref,
    out_ref,
    region, recv_pack, send_pack, chirp_w, chirp_c, left_f, left_b, right_f, right_b,
    prolled, stacked, halves, phi, second, gsend, gown, gpack, crecv, cpack, dsend, down, drecv,
    dhalf, send_sem, recv_sem,
):
    row = lax.axis_index("row")
    col = lax.axis_index("col")
    half = tile // 2
    n = length
    rows_all = 4 * tile
    spot = {"row": (row, n_row), "col": (col, n_col)}

    def has(axis, step):
        at, count = spot[axis]
        return jnp.logical_and(at + step >= 0, at + step < count)

    barrier = pltpu.get_barrier_semaphore()
    peers = jnp.int32(0)
    for axis in ("row", "col"):
        for step in STEPS:
            there = has(axis, step)
            peers = peers + there.astype(jnp.int32)

            @pl.when(there)
            def _(axis=axis, step=step):
                pl.semaphore_signal(
                    barrier, inc=1, device_id={axis: spot[axis][0] + step}, device_id_type=MESH
                )

    pl.semaphore_wait(barrier, peers)

    def endpoints(phase, s):
        if phase == 0:
            ends = (
                (obj_ref.at[s, :, 0:half], region.at[s, 1, :, 3 * tile:3 * tile + half]),
                (obj_ref.at[s], region.at[s, 1, :, 2 * tile:3 * tile]),
                (obj_ref.at[s], region.at[s, 1, :, 0:tile]),
                (obj_ref.at[s, :, half:tile], region.at[s, 1, :, 3 * tile + half:4 * tile]),
            )
        elif phase == 1:
            ends = (
                (send_pack.at[s, 1], recv_pack.at[s, 0]),
                (region.at[s, 1], region.at[s, 2]),
                (region.at[s, 1], region.at[s, 0]),
                (send_pack.at[s, 0], recv_pack.at[s, 1]),
            )
        elif phase == 2:
            ends = (
                (gpack.at[s, 1], cpack.at[s, 1]),
                (gsend.at[s, 0], crecv.at[s, 0]),
                (gsend.at[s, 1], crecv.at[s, 1]),
                (gpack.at[s, 0], cpack.at[s, 0]),
            )
        else:
            ends = (
                (dsend.at[s, :, 3 * tile + half:4 * tile], dhalf.at[s, 1]),
                (dsend.at[s, :, 0:tile], drecv.at[s, 0]),
                (dsend.at[s, :, 2 * tile:3 * tile], drecv.at[s, 1]),
                (dsend.at[s, :, 3 * tile:3 * tile + half], dhalf.at[s, 0]),
            )
        return "col" if phase in (1, 2) else "row", ends

    def descriptors(phase, s):
        axis, ends = endpoints(phase, s)
        made = []
        for k, step in enumerate(STEPS):
            made.append(
                pltpu.make_async_remote_copy(
                    src_ref=ends[k][0],
                    dst_ref=ends[k][1],
                    send_sem=send_sem.at[phase, s, k],
                    recv_sem=recv_sem.at[phase, s, k],
                    device_id={axis: spot[axis][0] + step},
                    device_id_type=MESH,
                )
            )
        return axis, made

    def start(phase, s):
        axis, made = descriptors(phase, s)
        for step, copy in sorted(zip(STEPS, made), key=lambda pair: -abs(pair[0])):
            @pl.when(has(axis, step))
            def _(copy=copy):
                copy.start()

    def wait_recv(phase, s):
        axis, made = descriptors(phase, s)
        for k, step in enumerate(STEPS):
            @pl.when(has(axis, -step))
            def _(copy=made[k]):
                copy.wait_recv()

    def wait_send(phase, s):
        axis, made = descriptors(phase, s)
        for step, copy in zip(STEPS, made):
            @pl.when(has(axis, step))
            def _(copy=copy):
                copy.wait_send()

    def clear(phase, s):
        axis, ends = endpoints(phase, s)
        for k, step in enumerate(STEPS):
            @pl.when(jnp.logical_not(has(axis, -step)))
            def _(target=ends[k][1]):
                target[...] = jnp.zeros(target.shape, target.dtype)

    start(0, 0)
    start(0, 1)
    for phase in range(4):
        for s in range(2):
            clear(phase, s)

    u = offs_ref[0]
    v = offs_ref[1]
    shift_u = lax.rem(u + n - half, n)
    shift_v = lax.rem(v + n - half, n)

    def pack(re, im, left):
        lane = lax.broadcasted_iota(jnp.int32, re.shape, 1)
        moved = pltpu.roll(im, half, 1)
        return jnp.where(lane < half, re, moved) if left else jnp.where(lane < half, moved, re)

    def unpack(packed):
        return packed, pltpu.roll(packed, half, 1)

    region[0, 1, :, tile:2 * tile] = obj_ref[0]
    region[1, 1, :, tile:2 * tile] = obj_ref[1]

    def second_phase(s):
        wait_recv(0, s)
        re = region[s, 1, 0].astype(F32)
        im = region[s, 1, 1].astype(F32)
        send_pack[s, 0] = pack(re, im, False).astype(BF16)
        send_pack[s, 1] = pack(re, im, True).astype(BF16)
        start(1, s)

    def fill(target, a, b, c, d):
        target[0:n, 0:n] = a
        target[0:n, n:2 * n] = b
        target[n:2 * n, 0:n] = c
        target[n:2 * n, n:2 * n] = d

    for k in range(2):
        prolled[k] = pltpu.roll(pltpu.roll(probe_ref[k], shift_u, 0), shift_v, 1)
    second_phase(0)
    hre, him = hre_ref[...], him_ref[...]
    fill(chirp_w, hre, him, -him, hre)
    fill(chirp_c, hre, -him, him, hre)
    second_phase(1)
    fre, fim = fre_ref[...].astype(F32), fim_ref[...].astype(F32)

    def rolled(shift, axis):
        return pltpu.roll(fre, shift, axis).astype(BF16), pltpu.roll(fim, shift, axis).astype(BF16)

    re, im = rolled(shift_u, 1)
    fill(left_f, re, -im, im, re)
    re, im = rolled(shift_u, 0)
    fill(left_b, re, im, -im, re)
    re, im = rolled(shift_v, 0)
    fill(right_f, re, im, -im, re)
    re, im = rolled(shift_v, 1)
    fill(right_b, re, -im, im, re)

    row_half = lax.broadcasted_iota(jnp.int32, (half, tile), 0)
    lane_full = lax.broadcasted_iota(jnp.int32, (n, tile), 1)
    near_top = row_half >= u - half
    near_bottom = row_half + (n - half) < u + n - half
    near_left = lane_full >= v - half
    near_right = lane_full + 2 * tile < v + n - half

    def pick_rows(x):
        x = x.astype(F32)
        top = jnp.where(near_top, x[0:half], x[n:n + half])
        bottom = jnp.where(near_bottom, x[n - half:n], x[n + half:n + tile])
        return jnp.concatenate([top, x[half:n - half], bottom], axis=0)

    def spread_rows(x):
        top, bottom = x[0:half], x[n - half:n]
        zero = jnp.zeros_like(top)
        return jnp.concatenate(
            [
                jnp.where(near_top, top, zero), x[half:n - half], jnp.where(near_bottom, bottom, zero),
                jnp.where(near_top, zero, top), jnp.where(near_bottom, zero, bottom),
            ],
            axis=0,
        )

    def window(s):
        left_alt = unpack(pick_rows(recv_pack[s, 0]))
        right_alt = unpack(pick_rows(recv_pack[s, 1]))
        made = []
        for k in range(2):
            made.append((
                jnp.where(near_left, pick_rows(region[s, 0, k]), left_alt[k]),
                pick_rows(region[s, 1, k]),
                jnp.where(near_right, pick_rows(region[s, 2, k]), right_alt[k]),
            ))
        return made

    def left_mul(table):
        product = jnp.dot(table[...], stacked[...], preferred_element_type=F32)
        halves[:, 0:n] = product[0:n].astype(BF16)
        halves[:, n:2 * n] = product[n:2 * n].astype(BF16)

    def right_mul(table):
        product = jnp.dot(halves[...], table[...], preferred_element_type=F32)
        return product[:, 0:n], product[:, n:2 * n]

    def scatter_start(s, grad_re, grad_im):
        lefts, rights = [], []
        for k, grad in enumerate((grad_re, grad_im)):
            first, mid, last = grad[:, 0:tile], grad[:, tile:2 * tile], grad[:, 2 * tile:n]
            zero = jnp.zeros_like(first)
            gsend[s, 0, k] = spread_rows(jnp.where(near_left, first, zero)).astype(BF16)
            gsend[s, 1, k] = spread_rows(jnp.where(near_right, last, zero)).astype(BF16)
            gown[s, k] = spread_rows(mid)
            lefts.append(jnp.where(near_left, zero, first))
            rights.append(jnp.where(near_right, zero, last))
        gpack[s, 0] = spread_rows(pack(lefts[0], lefts[1], True)).astype(BF16)
        gpack[s, 1] = spread_rows(pack(rights[0], rights[1], False)).astype(BF16)
        start(2, s)

    def scatter_rows(s):
        wait_recv(2, s)
        lane = lax.broadcasted_iota(jnp.int32, (rows_all, tile), 1)
        lefts = unpack(cpack[s, 0].astype(F32))
        rights = unpack(cpack[s, 1].astype(F32))
        for k in range(2):
            total = gown[s, k] + crecv[s, 0, k].astype(F32) + crecv[s, 1, k].astype(F32)
            total = total + jnp.where(lane < half, lefts[k], rights[k])
            dsend[s, k] = total.astype(BF16)
            down[s, k] = total[tile:2 * tile]
        start(3, s)

    def finish(s):
        wait_recv(3, s)
        keep = owned_ref[0].astype(F32)
        for k in range(2):
            total = down[s, k] + drecv[s, 0, k].astype(F32) + drecv[s, 1, k].astype(F32)
            ends = jnp.concatenate([dhalf[s, 0, k], dhalf[s, 1, k]], axis=0).astype(F32)
            out_ref[s, k] = (total + ends) * keep

    wait_recv(1, 0)
    first_re, first_im = window(0)
    for k in range(3):
        lanes = slice(k * tile, (k + 1) * tile)
        probe_re, probe_im = prolled[0, :, lanes], prolled[1, :, lanes]
        a, b = first_re[k], first_im[k]
        stacked[0:n, lanes] = (probe_re * a - probe_im * b).astype(BF16)
        stacked[n:2 * n, lanes] = (probe_re * b + probe_im * a).astype(BF16)
    left_mul(chirp_c)
    phi_re, phi_im = right_mul(chirp_w)
    phi[0], phi[1] = phi_re, phi_im
    wait_recv(1, 1)
    second_re, second_im = window(1)
    for k in range(3):
        lanes = slice(k * tile, (k + 1) * tile)
        second[0, :, lanes], second[1, :, lanes] = second_re[k], second_im[k]
        a, b = second_re[k], second_im[k]
        p, q = phi[0, :, lanes], phi[1, :, lanes]
        stacked[0:n, lanes] = (p * a - q * b).astype(BF16)
        stacked[n:2 * n, lanes] = (p * b + q * a).astype(BF16)
    left_mul(left_f)
    wave_re, wave_im = right_mul(right_f)
    power = wave_re * wave_re + wave_im * wave_im
    ratio = meas_ref[...] * lax.rsqrt(jnp.maximum(power, 0.25))
    stacked[0:n] = (wave_re - ratio * wave_re).astype(BF16)
    stacked[n:2 * n] = (wave_im - ratio * wave_im).astype(BF16)
    left_mul(left_b)
    back_re, back_im = right_mul(right_b)
    p, q = phi[0], phi[1]
    scatter_start(1, p * back_re + q * back_im, p * back_im - q * back_re)
    a, b = second[0], second[1]
    stacked[0:n] = (a * back_re + b * back_im).astype(BF16)
    stacked[n:2 * n] = (a * back_im - b * back_re).astype(BF16)
    left_mul(chirp_w)
    front_re, front_im = right_mul(chirp_c)
    p, q = prolled[0], prolled[1]
    scatter_start(0, p * front_re + q * front_im, p * front_im - q * front_re)
    scatter_rows(1)
    scatter_rows(0)
    finish(1)
    finish(0)
    for phase in range(4):
        for s in range(2):
            wait_send(phase, s)


def shards(n_row, n_col, object_slices, probe, measured, offsets, owned):
    tile = object_slices.shape[2]
    length = probe.shape[1]
    tables = make_tables(length)
    rows_all = 4 * tile
    vmem = pl.BlockSpec(memory_space=pltpu.VMEM)
    smem = pl.BlockSpec(memory_space=pltpu.SMEM)
    wide = pltpu.VMEM((2 * length, 2 * length), BF16)
    packs = pltpu.VMEM((2, 2, rows_all, tile), BF16)
    return pl.pallas_call(
        functools.partial(kernel, n_row, n_col, tile, length),
        out_shape=jax.ShapeDtypeStruct(object_slices.shape, F32),
        in_specs=[smem, smem] + [vmem] * 7,
        out_specs=vmem,
        scratch_shapes=[
            pltpu.VMEM((2, 3, 2, rows_all, tile), BF16),
            packs, packs,
            wide, wide, wide, wide, wide, wide,
            pltpu.VMEM((2, length, length), F32),
            pltpu.VMEM((2 * length, length), BF16),
            pltpu.VMEM((length, 2 * length), BF16),
            pltpu.VMEM((2, length, length), F32),
            pltpu.VMEM((2, length, length), F32),
            pltpu.VMEM((2, 2, 2, rows_all, tile), BF16),
            pltpu.VMEM((2, 2, rows_all, tile), F32),
            packs,
            pltpu.VMEM((2, 2, 2, rows_all, tile), BF16),
            packs, packs,
            pltpu.VMEM((2, 2, tile, tile), F32),
            pltpu.VMEM((2, 2, 2, tile, tile), BF16),
            pltpu.VMEM((2, 2, 2, tile // 2, tile), BF16),
            pltpu.SemaphoreType.DMA((4, 2, 4)),
            pltpu.SemaphoreType.DMA((4, 2, 4)),
        ],
        compiler_params=pltpu.CompilerParams(
            collective_id=0, has_side_effects=True, vmem_limit_bytes=50 * 1024 * 1024
        ),
    )(
        offsets.reshape(2), owned.reshape(1), object_slices, probe,
        measured.reshape(length, length), *tables,
    )


def solution(mesh):
    in_specs = (
        P(None, None, ("groups", "row"), "col"),
        P(),
        P(("groups", "row"), "col", None, None, None),
        P(("groups", "row"), "col", None, None),
        P(("groups", "row"), "col"),
    )
    out_specs = P(None, None, ("groups", "row"), "col")
    body = functools.partial(shards, mesh.shape["row"], mesh.shape["col"])
    return jax.shard_map(body, mesh=mesh, in_specs=in_specs, out_specs=out_specs, check_vma=False)
```

time: 285 us -> 49.4 us (0.17)
  the two profiles are of different devices: /device:TPU:1 before, /device:TPU:6 now
where the time goes in v1:
time: 49.4 us; the launch traced here: 49 us
  Pallas kernels  39.9 us (81%)
  local copies, waits for them, and re-layouts  8.44 us (17%)
  between operations  0.68 us (1%)
    pallas_call x1, Pallas kernels, shards(): pl.pallas_call(functools.partial(kernel, n_row, n_col, tile, length), out...  39.9 us
    unnamed x17, local copies, waits for them, and re-layouts  8.44 us

profile of v1, /device:TPU:6, one launch (start us, length us, event | category | flops | bytes accessed | tf_op | source)
XLA Modules:
  0.0 49.0 jit_solution(10948287595659505745)
XLA Ops:
  0.7 0.0 copy-start
  0.7 1.3 %copy-done = f32[2,384,384]{2,1,0:T(8,128)S(1)} copy-done((f32[2,384,384]{2,1,0:T(8,128)S(1)}, f32[2,384,384]{2,1,0:T(8,128)}, u32[]{:S(2)}) %copy-start) | copy-done | bytes 1179672
  1.9 0.0 copy-start.1
  1.9 1.1 %copy-done.1 = f32[1,1,1,384,384]{4,3,2,1,0:T(8,128)S(1)} copy-done((f32[1,1,1,384,384]{4,3,2,1,0:T(8,128)S(1)}, f32[1,1,1,384,384]{4,3,2,1,0:T(8,128)}, u32[]{:S(2)}) %copy-start.1) | copy-done | bytes 589848
  3.0 0.0 copy-start.2
  3.0 1.0 %copy-done.2 = bf16[384,384]{1,0:T(8,128)(2,1)S(1)} copy-done((bf16[384,384]{1,0:T(8,128)(2,1)S(1)}, bf16[384,384]{1,0:T(8,128)(2,1)}, u32[]{:S(2)}) %copy-start.2) | copy-done | bytes 294936
  4.0 0.0 copy-start.3
  4.0 1.0 %copy-done.3 = bf16[384,384]{1,0:T(8,128)(2,1)S(1)} copy-done((bf16[384,384]{1,0:T(8,128)(2,1)S(1)}, bf16[384,384]{1,0:T(8,128)(2,1)}, u32[]{:S(2)}) %copy-start.3) | copy-done | bytes 294936
  4.9 0.0 copy-start.4
  4.9 1.0 %copy-done.4 = bf16[384,384]{1,0:T(8,128)(2,1)S(1)} copy-done((bf16[384,384]{1,0:T(8,128)(2,1)S(1)}, bf16[384,384]{1,0:T(8,128)(2,1)}, u32[]{:S(2)}) %copy-start.4) | copy-done | bytes 294936
  5.9 0.0 copy-start.5
  5.9 1.0 %copy-done.5 = bf16[384,384]{1,0:T(8,128)(2,1)S(1)} copy-done((bf16[384,384]{1,0:T(8,128)(2,1)S(1)}, bf16[384,384]{1,0:T(8,128)(2,1)}, u32[]{:S(2)}) %copy-start.5) | copy-done | bytes 294936
  6.8 0.0 copy-start.6
  6.8 0.9 %copy-done.6 = bf16[2,2,128,128]{3,2,1,0:T(8,128)(2,1)S(1)} copy-done((bf16[2,2,128,128]{3,2,1,0:T(8,128)(2,1)S(1)}, bf16[2,2,128,128]{3,2,1,0:T(8,128)(2,1)}, u32[]{:S(2)}) %copy-start.6) | copy-done | bytes 131096
  7.7 0.0 copy-start.7
  7.7 0.7 %copy-done.7 = s32[1,1,1,2]{3,2,1,0:T(1,128)S(1)} copy-done((s32[1,1,1,2]{3,2,1,0:T(1,128)S(1)}, s32[1,1,1,2]{3,2,1,0:T(1,128)}, u32[]{:S(2)}) %copy-start.7) | copy-done | bytes 32
  8.4 39.9 %shard_map.91 = f32[2,2,128,128]{3,2,1,0:T(8,128)S(1)} custom-call(s32[2]{0:T(128)S(1)} %bitcast.5, s32[1]{0:T(128)} %bitcast.3.owned_ref, bf16[2,2,128,128]{3,2,1,0:T(8,128)(2,1)S(1)} %copy-done.6, f32[2,384,384]{2,1,0:T(8,128)S(1)} %copy-done, f32[384,384]{1,0:T(8,128)S(1)} %bitcast.4, bf16[384,384]{1,0:T(8,128)(2,1)S(1)} %copy-done.5, ...), custom_call_target="tpu_custom_call" | custom-call | tf_op jit(solution)/shard_map/pallas_call | solution.py:329
  48.3 0.7 %copy.12 = f32[2,2,128,128]{3,2,1,0:T(8,128)} copy(f32[2,2,128,128]{3,2,1,0:T(8,128)S(1)} %shard_map.91) | data formatting | bytes 524288
Async XLA Ops:
  0.7 1.3 %copy-start = (f32[2,384,384]{2,1,0:T(8,128)S(1)}, f32[2,384,384]{2,1,0:T(8,128)}, u32[]{:S(2)}) copy-start(f32[2,384,384]{2,1,0:T(8,128)} %probe_ref.1) | copy-start | bytes 3538948
  1.9 1.1 %copy-start.1 = (f32[1,1,1,384,384]{4,3,2,1,0:T(8,128)S(1)}, f32[1,1,1,384,384]{4,3,2,1,0:T(8,128)}, u32[]{:S(2)}) copy-start(f32[1,1,1,384,384]{4,3,2,1,0:T(8,128)} %param.11) | copy-start | bytes 1769476
  3.0 1.0 %copy-start.2 = (bf16[384,384]{1,0:T(8,128)(2,1)S(1)}, bf16[384,384]{1,0:T(8,128)(2,1)}, u32[]{:S(2)}) copy-start(bf16[384,384]{1,0:T(8,128)(2,1)} %constant.11.clone.fim_ref) | copy-start | bytes 884740
  4.0 1.0 %copy-start.3 = (bf16[384,384]{1,0:T(8,128)(2,1)S(1)}, bf16[384,384]{1,0:T(8,128)(2,1)}, u32[]{:S(2)}) copy-start(bf16[384,384]{1,0:T(8,128)(2,1)} %constant.10.clone.fre_ref) | copy-start | bytes 884740
  4.9 1.0 %copy-start.4 = (bf16[384,384]{1,0:T(8,128)(2,1)S(1)}, bf16[384,384]{1,0:T(8,128)(2,1)}, u32[]{:S(2)}) copy-start(bf16[384,384]{1,0:T(8,128)(2,1)} %constant.9.clone.him_ref) | copy-start | bytes 884740
  5.9 1.0 %copy-start.5 = (bf16[384,384]{1,0:T(8,128)(2,1)S(1)}, bf16[384,384]{1,0:T(8,128)(2,1)}, u32[]{:S(2)}) copy-start(bf16[384,384]{1,0:T(8,128)(2,1)} %constant.8.clone.hre_ref) | copy-start | bytes 884740
  6.8 0.9 %copy-start.6 = (bf16[2,2,128,128]{3,2,1,0:T(8,128)(2,1)S(1)}, bf16[2,2,128,128]{3,2,1,0:T(8,128)(2,1)}, u32[]{:S(2)}) copy-start(bf16[2,2,128,128]{3,2,1,0:T(8,128)(2,1)} %obj_ref.1) | copy-start | bytes 393220
  7.7 0.7 %copy-start.7 = (s32[1,1,1,2]{3,2,1,0:T(1,128)S(1)}, s32[1,1,1,2]{3,2,1,0:T(1,128)}, u32[]{:S(2)}) copy-start(s32[1,1,1,2]{3,2,1,0:T(1,128)} %param.12) | copy-start | bytes 28

commit v2 on v1

--- a/solution.py
+++ b/solution.py
@@ -23,16 +23,16 @@
     fourier = product.astype(np.float32) * np.float32(-2.0 * math.pi / length)
     scaling = np.float32(1.0 / math.sqrt(length))
     parts = (np.cos(chirp), np.sin(chirp), np.cos(fourier), np.sin(fourier))
-    return [jnp.asarray(part * scaling, BF16) for part in parts]
+    return jnp.asarray(np.stack(parts) * scaling, BF16)
 
 
 def kernel(
     n_row, n_col, tile, length,
-    offs_ref, owned_ref, obj_ref, probe_ref, meas_ref, hre_ref, him_ref, fre_ref, fim_ref,
+    offs_ref, owned_ref, obj_ref, probe_hbm, meas_hbm, tables_hbm,
     out_ref,
-    region, recv_pack, send_pack, chirp_w, chirp_c, left_f, left_b, right_f, right_b,
+    probe_ref, meas_ref, tables_ref, region, recv_pack, send_pack, chirp_w, chirp_c, left_f, left_b, right_f, right_b,
     prolled, stacked, halves, phi, second, gsend, gown, gpack, crecv, cpack, dsend, down, drecv,
-    dhalf, send_sem, recv_sem,
+    dhalf, send_sem, recv_sem, load_sem,
 ):
     row = lax.axis_index("row")
     col = lax.axis_index("col")
@@ -44,6 +44,19 @@
     def has(axis, step):
         at, count = spot[axis]
         return jnp.logical_and(at + step >= 0, at + step < count)
+
+    loads = [
+        pltpu.make_async_copy(src, dst, load_sem.at[k])
+        for k, (src, dst) in enumerate((
+            (obj_ref.at[0], region.at[0, 1, :, tile:2 * tile]),
+            (obj_ref.at[1], region.at[1, 1, :, tile:2 * tile]),
+            (probe_hbm, probe_ref),
+            (tables_hbm, tables_ref),
+            (meas_hbm.at[0, 0, 0], meas_ref),
+        ))
+    ]
+    for load in loads:
+        load.start()
 
     barrier = pltpu.get_barrier_semaphore()
     peers = jnp.int32(0)
@@ -91,11 +104,12 @@
             )
         return "col" if phase in (1, 2) else "row", ends
 
-    def descriptors(phase, s):
+    def descriptors(phase, s, steps=STEPS):
         axis, ends = endpoints(phase, s)
-        made = []
-        for k, step in enumerate(STEPS):
-            made.append(
+        made = {}
+        for step in steps:
+            k = STEPS.index(step)
+            made[step] = (
                 pltpu.make_async_remote_copy(
                     src_ref=ends[k][0],
                     dst_ref=ends[k][1],
@@ -107,9 +121,11 @@
             )
         return axis, made
 
-    def start(phase, s):
-        axis, made = descriptors(phase, s)
-        for step, copy in sorted(zip(STEPS, made), key=lambda pair: -abs(pair[0])):
+    def start(phase, s, steps=(-2, 2, -1, 1)):
+        axis, made = descriptors(phase, s, steps)
+        for step in steps:
+            copy = made[step]
+
             @pl.when(has(axis, step))
             def _(copy=copy):
                 copy.start()
@@ -118,12 +134,12 @@
         axis, made = descriptors(phase, s)
         for k, step in enumerate(STEPS):
             @pl.when(has(axis, -step))
-            def _(copy=made[k]):
+            def _(copy=made[step]):
                 copy.wait_recv()
 
     def wait_send(phase, s):
         axis, made = descriptors(phase, s)
-        for step, copy in zip(STEPS, made):
+        for step, copy in made.items():
             @pl.when(has(axis, step))
             def _(copy=copy):
                 copy.wait_send()
@@ -136,13 +152,12 @@
                 target[...] = jnp.zeros(target.shape, target.dtype)
 
     start(0, 0)
-    start(0, 1)
-    for phase in range(4):
+    for phase in range(2):
         for s in range(2):
             clear(phase, s)
 
-    u = offs_ref[0]
-    v = offs_ref[1]
+    u = offs_ref[0, 0, 0, 0]
+    v = offs_ref[0, 0, 0, 1]
     shift_u = lax.rem(u + n - half, n)
     shift_v = lax.rem(v + n - half, n)
 
@@ -154,10 +169,8 @@
     def unpack(packed):
         return packed, pltpu.roll(packed, half, 1)
 
-    region[0, 1, :, tile:2 * tile] = obj_ref[0]
-    region[1, 1, :, tile:2 * tile] = obj_ref[1]
-
     def second_phase(s):
+        loads[s].wait()
         wait_recv(0, s)
         re = region[s, 1, 0].astype(F32)
         im = region[s, 1, 1].astype(F32)
@@ -171,14 +184,19 @@
         target[n:2 * n, 0:n] = c
         target[n:2 * n, n:2 * n] = d
 
+    loads[2].wait()
     for k in range(2):
         prolled[k] = pltpu.roll(pltpu.roll(probe_ref[k], shift_u, 0), shift_v, 1)
     second_phase(0)
-    hre, him = hre_ref[...], him_ref[...]
+    start(0, 1)
+    loads[3].wait()
+    hre, him = tables_ref[0], tables_ref[1]
     fill(chirp_w, hre, him, -him, hre)
     fill(chirp_c, hre, -him, him, hre)
-    second_phase(1)
-    fre, fim = fre_ref[...].astype(F32), fim_ref[...].astype(F32)
+    for phase in range(2, 4):
+        for s in range(2):
+            clear(phase, s)
+    fre, fim = tables_ref[2].astype(F32), tables_ref[3].astype(F32)
 
     def rolled(shift, axis):
         return pltpu.roll(fre, shift, axis).astype(BF16), pltpu.roll(fim, shift, axis).astype(BF16)
@@ -233,23 +251,24 @@
         halves[:, 0:n] = product[0:n].astype(BF16)
         halves[:, n:2 * n] = product[n:2 * n].astype(BF16)
 
-    def right_mul(table):
-        product = jnp.dot(halves[...], table[...], preferred_element_type=F32)
-        return product[:, 0:n], product[:, n:2 * n]
-
-    def scatter_start(s, grad_re, grad_im):
-        lefts, rights = [], []
-        for k, grad in enumerate((grad_re, grad_im)):
-            first, mid, last = grad[:, 0:tile], grad[:, tile:2 * tile], grad[:, 2 * tile:n]
-            zero = jnp.zeros_like(first)
-            gsend[s, 0, k] = spread_rows(jnp.where(near_left, first, zero)).astype(BF16)
-            gsend[s, 1, k] = spread_rows(jnp.where(near_right, last, zero)).astype(BF16)
-            gown[s, k] = spread_rows(mid)
-            lefts.append(jnp.where(near_left, zero, first))
-            rights.append(jnp.where(near_right, zero, last))
-        gpack[s, 0] = spread_rows(pack(lefts[0], lefts[1], True)).astype(BF16)
-        gpack[s, 1] = spread_rows(pack(rights[0], rights[1], False)).astype(BF16)
-        start(2, s)
+    def right_mul(table, k):
+        columns = [table[:, at:at + tile] for at in (k * tile, n + k * tile)]
+        product = jnp.dot(
+            halves[...], jnp.concatenate(columns, axis=1), preferred_element_type=F32
+        )
+        return product[:, 0:tile], product[:, tile:2 * tile]
+
+    def scatter_slot(s, k, grad_re, grad_im):
+        if k == 1:
+            gown[s, 0], gown[s, 1] = spread_rows(grad_re), spread_rows(grad_im)
+            return
+        near = near_left if k == 0 else near_right
+        zero = jnp.zeros_like(grad_re)
+        far = [jnp.where(near, zero, grad) for grad in (grad_re, grad_im)]
+        gpack[s, k // 2] = spread_rows(pack(far[0], far[1], k == 0)).astype(BF16)
+        for part, grad in enumerate((grad_re, grad_im)):
+            gsend[s, k // 2, part] = spread_rows(jnp.where(near, grad, zero)).astype(BF16)
+        start(2, s, (2, -1) if k == 0 else (-2, 1))
 
     def scatter_rows(s):
         wait_recv(2, s)
@@ -265,49 +284,55 @@
 
     def finish(s):
         wait_recv(3, s)
-        keep = owned_ref[0].astype(F32)
+        keep = owned_ref[0, 0].astype(F32)
         for k in range(2):
             total = down[s, k] + drecv[s, 0, k].astype(F32) + drecv[s, 1, k].astype(F32)
             ends = jnp.concatenate([dhalf[s, 0, k], dhalf[s, 1, k]], axis=0).astype(F32)
             out_ref[s, k] = (total + ends) * keep
 
+    def lanes_of(k):
+        return slice(k * tile, (k + 1) * tile)
+
+    def stack(k, re, im):
+        stacked[0:n, lanes_of(k)] = re.astype(BF16)
+        stacked[n:2 * n, lanes_of(k)] = im.astype(BF16)
+
     wait_recv(1, 0)
+    second_phase(1)
     first_re, first_im = window(0)
     for k in range(3):
-        lanes = slice(k * tile, (k + 1) * tile)
-        probe_re, probe_im = prolled[0, :, lanes], prolled[1, :, lanes]
+        p, q = prolled[0, :, lanes_of(k)], prolled[1, :, lanes_of(k)]
         a, b = first_re[k], first_im[k]
-        stacked[0:n, lanes] = (probe_re * a - probe_im * b).astype(BF16)
-        stacked[n:2 * n, lanes] = (probe_re * b + probe_im * a).astype(BF16)
+        stack(k, p * a - q * b, p * b + q * a)
     left_mul(chirp_c)
-    phi_re, phi_im = right_mul(chirp_w)
-    phi[0], phi[1] = phi_re, phi_im
+    for k in range(3):
+        phi[0, :, lanes_of(k)], phi[1, :, lanes_of(k)] = right_mul(chirp_w, k)
     wait_recv(1, 1)
     second_re, second_im = window(1)
     for k in range(3):
-        lanes = slice(k * tile, (k + 1) * tile)
-        second[0, :, lanes], second[1, :, lanes] = second_re[k], second_im[k]
         a, b = second_re[k], second_im[k]
-        p, q = phi[0, :, lanes], phi[1, :, lanes]
-        stacked[0:n, lanes] = (p * a - q * b).astype(BF16)
-        stacked[n:2 * n, lanes] = (p * b + q * a).astype(BF16)
+        second[0, :, lanes_of(k)], second[1, :, lanes_of(k)] = a, b
+        p, q = phi[0, :, lanes_of(k)], phi[1, :, lanes_of(k)]
+        stack(k, p * a - q * b, p * b + q * a)
     left_mul(left_f)
-    wave_re, wave_im = right_mul(right_f)
-    power = wave_re * wave_re + wave_im * wave_im
-    ratio = meas_ref[...] * lax.rsqrt(jnp.maximum(power, 0.25))
-    stacked[0:n] = (wave_re - ratio * wave_re).astype(BF16)
-    stacked[n:2 * n] = (wave_im - ratio * wave_im).astype(BF16)
+    loads[4].wait()
+    for k in range(3):
+        wave_re, wave_im = right_mul(right_f, k)
+        power = wave_re * wave_re + wave_im * wave_im
+        ratio = meas_ref[:, lanes_of(k)] * lax.rsqrt(jnp.maximum(power, 0.25))
+        stack(k, wave_re - ratio * wave_re, wave_im - ratio * wave_im)
     left_mul(left_b)
-    back_re, back_im = right_mul(right_b)
-    p, q = phi[0], phi[1]
-    scatter_start(1, p * back_re + q * back_im, p * back_im - q * back_re)
-    a, b = second[0], second[1]
-    stacked[0:n] = (a * back_re + b * back_im).astype(BF16)
-    stacked[n:2 * n] = (a * back_im - b * back_re).astype(BF16)
+    for k in (0, 2, 1):
+        back_re, back_im = right_mul(right_b, k)
+        p, q = phi[0, :, lanes_of(k)], phi[1, :, lanes_of(k)]
+        scatter_slot(1, k, p * back_re + q * back_im, p * back_im - q * back_re)
+        a, b = second[0, :, lanes_of(k)], second[1, :, lanes_of(k)]
+        stack(k, a * back_re + b * back_im, a * back_im - b * back_re)
     left_mul(chirp_w)
-    front_re, front_im = right_mul(chirp_c)
-    p, q = prolled[0], prolled[1]
-    scatter_start(0, p * front_re + q * front_im, p * front_im - q * front_re)
+    for k in (0, 2, 1):
+        front_re, front_im = right_mul(chirp_c, k)
+        p, q = prolled[0, :, lanes_of(k)], prolled[1, :, lanes_of(k)]
+        scatter_slot(0, k, p * front_re + q * front_im, p * front_im - q * front_re)
     scatter_rows(1)
     scatter_rows(0)
     finish(1)
@@ -323,15 +348,19 @@
     tables = make_tables(length)
     rows_all = 4 * tile
     vmem = pl.BlockSpec(memory_space=pltpu.VMEM)
+    hbm = pl.BlockSpec(memory_space=pltpu.HBM)
     smem = pl.BlockSpec(memory_space=pltpu.SMEM)
     wide = pltpu.VMEM((2 * length, 2 * length), BF16)
     packs = pltpu.VMEM((2, 2, rows_all, tile), BF16)
     return pl.pallas_call(
         functools.partial(kernel, n_row, n_col, tile, length),
         out_shape=jax.ShapeDtypeStruct(object_slices.shape, F32),
-        in_specs=[smem, smem] + [vmem] * 7,
+        in_specs=[smem, smem] + [hbm] * 4,
         out_specs=vmem,
         scratch_shapes=[
+            pltpu.VMEM((2, length, length), F32),
+            pltpu.VMEM((length, length), F32),
+            pltpu.VMEM((4, length, length), BF16),
             pltpu.VMEM((2, 3, 2, rows_all, tile), BF16),
             packs, packs,
             wide, wide, wide, wide, wide, wide,
@@ -350,13 +379,14 @@
             pltpu.VMEM((2, 2, 2, tile // 2, tile), BF16),
             pltpu.SemaphoreType.DMA((4, 2, 4)),
             pltpu.SemaphoreType.DMA((4, 2, 4)),
+            pltpu.SemaphoreType.DMA((5,)),
         ],
         compiler_params=pltpu.CompilerParams(
-            collective_id=0, has_side_effects=True, vmem_limit_bytes=50 * 1024 * 1024
+            collective_id=0, has_side_effects=True, vmem_limit_bytes=63 * 1024 * 1024
         ),
     )(
-        offsets.reshape(2), owned.reshape(1), object_slices, probe,
-        measured.reshape(length, length), *tables,
+        offsets, owned, object_slices, probe,
+        measured, tables,
     )
 
 

time: 49.4 us -> 46.4 us (0.939)
  the two profiles are of different devices: /device:TPU:6 before, /device:TPU:0 now
where the time goes in v2:
time: 46.4 us; the launch traced here: 46.3 us
  Pallas kernels  44 us (95%)
  local copies, waits for them, and re-layouts  1.67 us (4%)
  between operations  0.66 us (1%)
    pallas_call x1, Pallas kernels, shards(): pl.pallas_call(functools.partial(kernel, n_row, n_col, tile, length), out...  44 us
    unnamed x1, local copies, waits for them, and re-layouts  1.67 us

profile of v2, /device:TPU:0, one launch (start us, length us, event | category | flops | bytes accessed | tf_op | source)
XLA Modules:
  0.0 46.3 jit_solution(16875058216861269080)
XLA Ops:
  0.7 44.0 %shard_map.64 = f32[2,2,128,128]{3,2,1,0:T(8,128)} custom-call(s32[1,1,1,2]{3,2,1,0:T(1,128)} %offs_ref.1, s32[1,1]{1,0:T(1,128)S(6)} %copy.8.owned_ref, bf16[2,2,128,128]{3,2,1,0:T(8,128)(2,1)} %obj_ref.1, f32[2,384,384]{2,1,0:T(8,128)} %probe_hbm.1, f32[1,1,1,384,384]{4,3,2,1,0:T(8,128)} %meas_hbm.1, bf16[4,384,384]{2,1,0:T(8,128)(2,1)} %constant.2.clone.tables_hbm), custom_call_target="tpu_custom_call" | custom-call | tf_op jit(solution)/shard_map/pallas_call | solution.py:355
  44.6 1.7 %copy.9 = f32[2,2,128,128]{3,2,1,0:T(8,128)} copy(f32[2,2,128,128]{3,2,1,0:T(8,128)} %shard_map.64) | data formatting | bytes 524288

commit v3 on v2

--- a/solution.py
+++ b/solution.py
@@ -30,7 +30,7 @@
     n_row, n_col, tile, length,
     offs_ref, owned_ref, obj_ref, probe_hbm, meas_hbm, tables_hbm,
     out_ref,
-    probe_ref, meas_ref, tables_ref, region, recv_pack, send_pack, chirp_w, chirp_c, left_f, left_b, right_f, right_b,
+    probe_ref, meas_ref, tables_ref, own_top, peer_top, strip, side_send, sides, recv_pack, send_pack, chirp_w, chirp_c, left_f, left_b, right_f, right_b,
     prolled, stacked, halves, phi, second, gsend, gown, gpack, crecv, cpack, dsend, down, drecv,
     dhalf, send_sem, recv_sem, load_sem,
 ):
@@ -48,8 +48,8 @@
     loads = [
         pltpu.make_async_copy(src, dst, load_sem.at[k])
         for k, (src, dst) in enumerate((
-            (obj_ref.at[0], region.at[0, 1, :, tile:2 * tile]),
-            (obj_ref.at[1], region.at[1, 1, :, tile:2 * tile]),
+            (obj_ref.at[0], strip.at[0, :, tile:2 * tile]),
+            (obj_ref.at[1], strip.at[1, :, tile:2 * tile]),
             (probe_hbm, probe_ref),
             (tables_hbm, tables_ref),
             (meas_hbm.at[0, 0, 0], meas_ref),
@@ -76,16 +76,16 @@
     def endpoints(phase, s):
         if phase == 0:
             ends = (
-                (obj_ref.at[s, :, 0:half], region.at[s, 1, :, 3 * tile:3 * tile + half]),
-                (obj_ref.at[s], region.at[s, 1, :, 2 * tile:3 * tile]),
-                (obj_ref.at[s], region.at[s, 1, :, 0:tile]),
-                (obj_ref.at[s, :, half:tile], region.at[s, 1, :, 3 * tile + half:4 * tile]),
+                (obj_ref.at[s, :, 0:half], strip.at[s, :, 3 * tile:3 * tile + half]),
+                (obj_ref.at[s], strip.at[s, :, 2 * tile:3 * tile]),
+                (obj_ref.at[s], strip.at[s, :, 0:tile]),
+                (obj_ref.at[s, :, half:tile], strip.at[s, :, 3 * tile + half:4 * tile]),
             )
         elif phase == 1:
             ends = (
                 (send_pack.at[s, 1], recv_pack.at[s, 0]),
-                (region.at[s, 1], region.at[s, 2]),
-                (region.at[s, 1], region.at[s, 0]),
+                (side_send.at[s, 0], sides.at[s, 1]),
+                (side_send.at[s, 1], sides.at[s, 0]),
                 (send_pack.at[s, 0], recv_pack.at[s, 1]),
             )
         elif phase == 2:
@@ -95,6 +95,8 @@
                 (gsend.at[s, 1], crecv.at[s, 1]),
                 (gpack.at[s, 0], cpack.at[s, 0]),
             )
+        elif phase == 4:
+            ends = tuple((own_top, peer_top.at[3 - k]) for k in range(4))
         else:
             ends = (
                 (dsend.at[s, :, 3 * tile + half:4 * tile], dhalf.at[s, 1]),
@@ -102,7 +104,7 @@
                 (dsend.at[s, :, 2 * tile:3 * tile], drecv.at[s, 1]),
                 (dsend.at[s, :, 3 * tile:3 * tile + half], dhalf.at[s, 0]),
             )
-        return "col" if phase in (1, 2) else "row", ends
+        return "col" if phase in (1, 2, 4) else "row", ends
 
     def descriptors(phase, s, steps=STEPS):
         axis, ends = endpoints(phase, s)
@@ -152,12 +154,14 @@
                 target[...] = jnp.zeros(target.shape, target.dtype)
 
     start(0, 0)
+    u = offs_ref[0, 0, 0, 0]
+    v = offs_ref[0, 0, 0, 1]
+    own_top[...] = jnp.full(own_top.shape, u.astype(F32))
+    start(4, 0)
+    clear(4, 0)
     for phase in range(2):
         for s in range(2):
             clear(phase, s)
-
-    u = offs_ref[0, 0, 0, 0]
-    v = offs_ref[0, 0, 0, 1]
     shift_u = lax.rem(u + n - half, n)
     shift_v = lax.rem(v + n - half, n)
 
@@ -169,14 +173,40 @@
     def unpack(packed):
         return packed, pltpu.roll(packed, half, 1)
 
-    def second_phase(s):
+    row_half = lax.broadcasted_iota(jnp.int32, (half, tile), 0).astype(F32)
+
+    def row_masks(top):
+        return row_half >= top - half, row_half < top
+
+    def pick_rows(x, masks):
+        top = jnp.where(masks[0], x[0:half], x[n:n + half])
+        bottom = jnp.where(masks[1], x[n - half:n], x[n + half:n + tile])
+        return jnp.concatenate([top, x[half:n - half], bottom], axis=0)
+
+    def spread_rows(x, masks):
+        top, bottom = x[0:half], x[n - half:n]
+        zero = jnp.zeros_like(top)
+        return jnp.concatenate(
+            [
+                jnp.where(masks[0], top, zero), x[half:n - half], jnp.where(masks[1], bottom, zero),
+                jnp.where(masks[0], zero, top), jnp.where(masks[1], zero, bottom),
+            ],
+            axis=0,
+        )
+
+    def second_phase(s, peer_masks):
         loads[s].wait()
         wait_recv(0, s)
-        re = region[s, 1, 0].astype(F32)
-        im = region[s, 1, 1].astype(F32)
-        send_pack[s, 0] = pack(re, im, False).astype(BF16)
-        send_pack[s, 1] = pack(re, im, True).astype(BF16)
-        start(1, s)
+        re = strip[s, 0].astype(F32)
+        im = strip[s, 1].astype(F32)
+        packed = {2: (pack(re, im, False), 0), -2: (pack(re, im, True), 1)}
+        for step in (2, -2):
+            send_pack[s, packed[step][1]] = pick_rows(packed[step][0], peer_masks[step]).astype(BF16)
+            start(1, s, (step,))
+        for side, step in enumerate((-1, 1)):
+            side_send[s, side, 0] = pick_rows(re, peer_masks[step]).astype(BF16)
+            side_send[s, side, 1] = pick_rows(im, peer_masks[step]).astype(BF16)
+            start(1, s, (step,))
 
     def fill(target, a, b, c, d):
         target[0:n, 0:n] = a
@@ -187,7 +217,10 @@
     loads[2].wait()
     for k in range(2):
         prolled[k] = pltpu.roll(pltpu.roll(probe_ref[k], shift_u, 0), shift_v, 1)
-    second_phase(0)
+    own_masks = row_masks(own_top[0:1])
+    wait_recv(4, 0)
+    peer_masks = {step: row_masks(peer_top[k, 0:1]) for k, step in enumerate(STEPS)}
+    second_phase(0, peer_masks)
     start(0, 1)
     loads[3].wait()
     hre, him = tables_ref[0], tables_ref[1]
@@ -210,39 +243,19 @@
     re, im = rolled(shift_v, 1)
     fill(right_b, re, -im, im, re)
 
-    row_half = lax.broadcasted_iota(jnp.int32, (half, tile), 0)
     lane_full = lax.broadcasted_iota(jnp.int32, (n, tile), 1)
-    near_top = row_half >= u - half
-    near_bottom = row_half + (n - half) < u + n - half
     near_left = lane_full >= v - half
     near_right = lane_full + 2 * tile < v + n - half
 
-    def pick_rows(x):
-        x = x.astype(F32)
-        top = jnp.where(near_top, x[0:half], x[n:n + half])
-        bottom = jnp.where(near_bottom, x[n - half:n], x[n + half:n + tile])
-        return jnp.concatenate([top, x[half:n - half], bottom], axis=0)
-
-    def spread_rows(x):
-        top, bottom = x[0:half], x[n - half:n]
-        zero = jnp.zeros_like(top)
-        return jnp.concatenate(
-            [
-                jnp.where(near_top, top, zero), x[half:n - half], jnp.where(near_bottom, bottom, zero),
-                jnp.where(near_top, zero, top), jnp.where(near_bottom, zero, bottom),
-            ],
-            axis=0,
-        )
-
     def window(s):
-        left_alt = unpack(pick_rows(recv_pack[s, 0]))
-        right_alt = unpack(pick_rows(recv_pack[s, 1]))
+        left_alt = unpack(recv_pack[s, 0].astype(F32))
+        right_alt = unpack(recv_pack[s, 1].astype(F32))
         made = []
         for k in range(2):
             made.append((
-                jnp.where(near_left, pick_rows(region[s, 0, k]), left_alt[k]),
-                pick_rows(region[s, 1, k]),
-                jnp.where(near_right, pick_rows(region[s, 2, k]), right_alt[k]),
+                jnp.where(near_left, sides[s, 0, k].astype(F32), left_alt[k]),
+                pick_rows(strip[s, k].astype(F32), own_masks),
+                jnp.where(near_right, sides[s, 1, k].astype(F32), right_alt[k]),
             ))
         return made
 
@@ -260,23 +273,25 @@
 
     def scatter_slot(s, k, grad_re, grad_im):
         if k == 1:
-            gown[s, 0], gown[s, 1] = spread_rows(grad_re), spread_rows(grad_im)
+            gown[s, 0], gown[s, 1] = grad_re, grad_im
             return
         near = near_left if k == 0 else near_right
         zero = jnp.zeros_like(grad_re)
         far = [jnp.where(near, zero, grad) for grad in (grad_re, grad_im)]
-        gpack[s, k // 2] = spread_rows(pack(far[0], far[1], k == 0)).astype(BF16)
+        gpack[s, k // 2] = pack(far[0], far[1], k == 0).astype(BF16)
         for part, grad in enumerate((grad_re, grad_im)):
-            gsend[s, k // 2, part] = spread_rows(jnp.where(near, grad, zero)).astype(BF16)
+            gsend[s, k // 2, part] = jnp.where(near, grad, zero).astype(BF16)
         start(2, s, (2, -1) if k == 0 else (-2, 1))
 
     def scatter_rows(s):
         wait_recv(2, s)
         lane = lax.broadcasted_iota(jnp.int32, (rows_all, tile), 1)
-        lefts = unpack(cpack[s, 0].astype(F32))
-        rights = unpack(cpack[s, 1].astype(F32))
+        lefts = unpack(spread_rows(cpack[s, 0].astype(F32), peer_masks[-2]))
+        rights = unpack(spread_rows(cpack[s, 1].astype(F32), peer_masks[2]))
         for k in range(2):
-            total = gown[s, k] + crecv[s, 0, k].astype(F32) + crecv[s, 1, k].astype(F32)
+            total = spread_rows(gown[s, k], own_masks)
+            total = total + spread_rows(crecv[s, 0, k].astype(F32), peer_masks[1])
+            total = total + spread_rows(crecv[s, 1, k].astype(F32), peer_masks[-1])
             total = total + jnp.where(lane < half, lefts[k], rights[k])
             dsend[s, k] = total.astype(BF16)
             down[s, k] = total[tile:2 * tile]
@@ -298,7 +313,7 @@
         stacked[n:2 * n, lanes_of(k)] = im.astype(BF16)
 
     wait_recv(1, 0)
-    second_phase(1)
+    second_phase(1, peer_masks)
     first_re, first_im = window(0)
     for k in range(3):
         p, q = prolled[0, :, lanes_of(k)], prolled[1, :, lanes_of(k)]
@@ -340,6 +355,7 @@
     for phase in range(4):
         for s in range(2):
             wait_send(phase, s)
+    wait_send(4, 0)
 
 
 def shards(n_row, n_col, object_slices, probe, measured, offsets, owned):
@@ -351,7 +367,8 @@
     hbm = pl.BlockSpec(memory_space=pltpu.HBM)
     smem = pl.BlockSpec(memory_space=pltpu.SMEM)
     wide = pltpu.VMEM((2 * length, 2 * length), BF16)
-    packs = pltpu.VMEM((2, 2, rows_all, tile), BF16)
+    packs = pltpu.VMEM((2, 2, length, tile), BF16)
+    sides = pltpu.VMEM((2, 2, 2, length, tile), BF16)
     return pl.pallas_call(
         functools.partial(kernel, n_row, n_col, tile, length),
         out_shape=jax.ShapeDtypeStruct(object_slices.shape, F32),
@@ -361,24 +378,25 @@
             pltpu.VMEM((2, length, length), F32),
             pltpu.VMEM((length, length), F32),
             pltpu.VMEM((4, length, length), BF16),
-            pltpu.VMEM((2, 3, 2, rows_all, tile), BF16),
-            packs, packs,
+            pltpu.VMEM((8, tile), F32),
+            pltpu.VMEM((4, 8, tile), F32),
+            pltpu.VMEM((2, 2, rows_all, tile), BF16),
+            sides, sides, packs, packs,
             wide, wide, wide, wide, wide, wide,
             pltpu.VMEM((2, length, length), F32),
             pltpu.VMEM((2 * length, length), BF16),
             pltpu.VMEM((length, 2 * length), BF16),
             pltpu.VMEM((2, length, length), F32),
             pltpu.VMEM((2, length, length), F32),
-            pltpu.VMEM((2, 2, 2, rows_all, tile), BF16),
-            pltpu.VMEM((2, 2, rows_all, tile), F32),
-            packs,
-            pltpu.VMEM((2, 2, 2, rows_all, tile), BF16),
-            packs, packs,
+            sides,
+            pltpu.VMEM((2, 2, length, tile), F32),
+            packs, sides, packs,
+            pltpu.VMEM((2, 2, rows_all, tile), BF16),
             pltpu.VMEM((2, 2, tile, tile), F32),
             pltpu.VMEM((2, 2, 2, tile, tile), BF16),
             pltpu.VMEM((2, 2, 2, tile // 2, tile), BF16),
-            pltpu.SemaphoreType.DMA((4, 2, 4)),
-            pltpu.SemaphoreType.DMA((4, 2, 4)),
+            pltpu.SemaphoreType.DMA((5, 2, 4)),
+            pltpu.SemaphoreType.DMA((5, 2, 4)),
             pltpu.SemaphoreType.DMA((5,)),
         ],
         compiler_params=pltpu.CompilerParams(

time: 46.4 us -> 42.4 us (0.914)
  Pallas kernels: 44 us -> 39.9 us
    pallas_call x1, Pallas kernels: 44 us -> 39.9 us  [shards(): pl.pallas_call(functools.partial(kernel, n_row, n_col, tile, length), out...]
where the time goes in v3:
time: 42.4 us; the launch traced here: 42.3 us
  Pallas kernels  39.9 us (94%)
  local copies, waits for them, and re-layouts  1.67 us (4%)
  between operations  0.66 us (2%)
    pallas_call x1, Pallas kernels, shards(): pl.pallas_call(functools.partial(kernel, n_row, n_col, tile, length), out...  39.9 us
    unnamed x1, local copies, waits for them, and re-layouts  1.67 us

profile of v3, /device:TPU:0, one launch (start us, length us, event | category | flops | bytes accessed | tf_op | source)
XLA Modules:
  0.0 42.3 jit_solution(15792933971901120185)
XLA Ops:
  0.7 39.9 %shard_map.64 = f32[2,2,128,128]{3,2,1,0:T(8,128)} custom-call(s32[1,1,1,2]{3,2,1,0:T(1,128)} %offs_ref.1, s32[1,1]{1,0:T(1,128)S(6)} %copy.8.owned_ref, bf16[2,2,128,128]{3,2,1,0:T(8,128)(2,1)} %obj_ref.1, f32[2,384,384]{2,1,0:T(8,128)} %probe_hbm.1, f32[1,1,1,384,384]{4,3,2,1,0:T(8,128)} %meas_hbm.1, bf16[4,384,384]{2,1,0:T(8,128)(2,1)} %constant.2.clone.tables_hbm), custom_call_target="tpu_custom_call" | custom-call | tf_op jit(solution)/shard_map/pallas_call | solution.py:372
  40.6 1.7 %copy.9 = f32[2,2,128,128]{3,2,1,0:T(8,128)} copy(f32[2,2,128,128]{3,2,1,0:T(8,128)} %shard_map.64) | data formatting | bytes 524288

commit v4 on v3

--- a/solution.py
+++ b/solution.py
@@ -312,8 +312,8 @@
         stacked[0:n, lanes_of(k)] = re.astype(BF16)
         stacked[n:2 * n, lanes_of(k)] = im.astype(BF16)
 
+    second_phase(1, peer_masks)
     wait_recv(1, 0)
-    second_phase(1, peer_masks)
     first_re, first_im = window(0)
     for k in range(3):
         p, q = prolled[0, :, lanes_of(k)], prolled[1, :, lanes_of(k)]

time: 42.4 us -> 39.4 us (0.929)
  Pallas kernels: 39.9 us -> 36.9 us
    pallas_call x1, Pallas kernels: 39.9 us -> 36.9 us  [shards(): pl.pallas_call(functools.partial(kernel, n_row, n_col, tile, length), out...]
where the time goes in v4:
time: 39.4 us; the launch traced here: 39.3 us
  Pallas kernels  36.9 us (94%)
  local copies, waits for them, and re-layouts  1.67 us (4%)
  between operations  0.66 us (2%)
    pallas_call x1, Pallas kernels, shards(): pl.pallas_call(functools.partial(kernel, n_row, n_col, tile, length), out...  36.9 us
    unnamed x1, local copies, waits for them, and re-layouts  1.67 us

profile of v4, /device:TPU:0, one launch (start us, length us, event | category | flops | bytes accessed | tf_op | source)
XLA Modules:
  0.0 39.3 jit_solution(8579164772593604309)
XLA Ops:
  0.7 36.9 %shard_map.64 = f32[2,2,128,128]{3,2,1,0:T(8,128)} custom-call(s32[1,1,1,2]{3,2,1,0:T(1,128)} %offs_ref.1, s32[1,1]{1,0:T(1,128)S(6)} %copy.8.owned_ref, bf16[2,2,128,128]{3,2,1,0:T(8,128)(2,1)} %obj_ref.1, f32[2,384,384]{2,1,0:T(8,128)} %probe_hbm.1, f32[1,1,1,384,384]{4,3,2,1,0:T(8,128)} %meas_hbm.1, bf16[4,384,384]{2,1,0:T(8,128)(2,1)} %constant.2.clone.tables_hbm), custom_call_target="tpu_custom_call" | custom-call | tf_op jit(solution)/shard_map/pallas_call | solution.py:372
  37.6 1.7 %copy.9 = f32[2,2,128,128]{3,2,1,0:T(8,128)} copy(f32[2,2,128,128]{3,2,1,0:T(8,128)} %shard_map.64) | data formatting | bytes 524288

commit v5 on v4

--- a/solution.py
+++ b/solution.py
@@ -288,14 +288,22 @@
         lane = lax.broadcasted_iota(jnp.int32, (rows_all, tile), 1)
         lefts = unpack(spread_rows(cpack[s, 0].astype(F32), peer_masks[-2]))
         rights = unpack(spread_rows(cpack[s, 1].astype(F32), peer_masks[2]))
+        totals = []
         for k in range(2):
             total = spread_rows(gown[s, k], own_masks)
             total = total + spread_rows(crecv[s, 0, k].astype(F32), peer_masks[1])
             total = total + spread_rows(crecv[s, 1, k].astype(F32), peer_masks[-1])
             total = total + jnp.where(lane < half, lefts[k], rights[k])
-            dsend[s, k] = total.astype(BF16)
-            down[s, k] = total[tile:2 * tile]
-        start(3, s)
+            totals.append(total)
+        for low, high, step in (
+            (3 * tile, 3 * tile + half, 2), (3 * tile + half, 4 * tile, -2),
+            (0, tile, -1), (2 * tile, 3 * tile, 1),
+        ):
+            for k in range(2):
+                dsend[s, k, low:high] = totals[k][low:high].astype(BF16)
+            start(3, s, (step,))
+        for k in range(2):
+            down[s, k] = totals[k][tile:2 * tile]
 
     def finish(s):
         wait_recv(3, s)

time: 39.4 us -> 39.4 us (level)
  no operation moved by 1% of the time
where the time goes in v5:
time: 39.4 us; the launch traced here: 39.3 us
  Pallas kernels  36.9 us (94%)
  local copies, waits for them, and re-layouts  1.67 us (4%)
  between operations  0.66 us (2%)
    pallas_call x1, Pallas kernels, shards(): pl.pallas_call(functools.partial(kernel, n_row, n_col, tile, length), out...  36.9 us
    unnamed x1, local copies, waits for them, and re-layouts  1.67 us

profile of v5, /device:TPU:0, one launch (start us, length us, event | category | flops | bytes accessed | tf_op | source)
XLA Modules:
  0.0 39.3 jit_solution(15494565173404656960)
XLA Ops:
  0.7 36.9 %shard_map.64 = f32[2,2,128,128]{3,2,1,0:T(8,128)} custom-call(s32[1,1,1,2]{3,2,1,0:T(1,128)} %offs_ref.1, s32[1,1]{1,0:T(1,128)S(6)} %copy.8.owned_ref, bf16[2,2,128,128]{3,2,1,0:T(8,128)(2,1)} %obj_ref.1, f32[2,384,384]{2,1,0:T(8,128)} %probe_hbm.1, f32[1,1,1,384,384]{4,3,2,1,0:T(8,128)} %meas_hbm.1, bf16[4,384,384]{2,1,0:T(8,128)(2,1)} %constant.2.clone.tables_hbm), custom_call_target="tpu_custom_call" | custom-call | tf_op jit(solution)/shard_map/pallas_call | solution.py:380
  37.6 1.7 %copy.9 = f32[2,2,128,128]{3,2,1,0:T(8,128)} copy(f32[2,2,128,128]{3,2,1,0:T(8,128)} %shard_map.64) | data formatting | bytes 524288
